TPU v7x, 256 devices: a whole 4x4x8 slice. The times are simulated.
256 devices in a mesh: band: 4 (over z_hi), slab: 64 (over y, x, z_lo, core).
Axes of the slice: x: 4, y: 4, z: 8 (z_hi: 4, z_lo: 2; z = z_hi * 2 + z_lo), core: 2. Of those that a mesh axis runs over, the one named last changes fastest.
Arguments:
- orbitals: float32 [2, 64, 128, 128, 128], P(None, 'band', 'slab'), may hold values from -6 to 6
- occupations: float32 [64], P('band'), may hold values from 0.01 to 0.1
- rest_density: float32 [128, 128, 128], P('slab'), may hold values from 1 to 8
- ionic_potential: float32 [128, 128, 128], P('slab'), may hold values from -6 to 6
Outputs:
- taylor_term: float32 [2, 64, 128, 128, 128], P(None, 'band', 'slab')
- potential: float32 [128, 128, 128], P('slab')
All inputs are finite; a program needn't handle non-finite values.
Results may differ from a plain program's by a relative error of at most 0.0003.
Values sent between devices are 32-bit elements; how exact they have to be, the bound alone decides.
A program may use at most 64 MiB of HBM per device.

v0:
```python
import functools
import math

import jax
import jax.numpy as jnp
import numpy as np
from jax import lax
from jax.experimental import pallas as pl
from jax.experimental.pallas import tpu as pltpu
from jax.sharding import PartitionSpec as P

MESH = pl.DeviceIdType.MESH
grid_spacing = 0.4
time_step = 0.01
exchange_factor = (3.0 / math.pi) ** (1.0 / 3.0)
CHUNKS = 4


def wavenumbers_squared(points):
    indices = np.arange(points)
    signed = np.where(indices < points // 2, indices, indices - points)
    return (2.0 * math.pi / (points * grid_spacing) * signed) ** 2


def real_basis(points):
    j = np.arange(points)[:, None]
    x = np.arange(points)[None, :]
    cosine = np.cos(2.0 * math.pi * (j * x % points) / points)
    sine = np.sin(2.0 * math.pi * ((points - j) * x % points) / points)
    rows = np.where(j <= points // 2, cosine, sine) * math.sqrt(2.0 / points)
    return np.where((j == 0) | (j == points // 2), rows * math.sqrt(0.5), rows)


def kinetic_matrix(points):
    basis = real_basis(points)
    return basis.T @ (0.5 * wavenumbers_squared(points)[:, None] * basis)


def split(values):
    high = values.astype(jnp.bfloat16)
    return high, (values - high.astype(jnp.float32)).astype(jnp.bfloat16)


def dot(a, b):
    return jnp.dot(a, b, preferred_element_type=jnp.float32)


def left(matrix_high, matrix_low, values):
    high, low = split(values)
    return dot(jnp.concatenate([matrix_high, matrix_high], 1), jnp.concatenate([high, low], 0)) + dot(matrix_low, high)


def right(values, matrix_high, matrix_low):
    high, low = split(values)
    return dot(jnp.concatenate([high, low], 1), jnp.concatenate([matrix_high, matrix_high], 0)) + dot(high, matrix_low)


def exact(a, b):
    return jnp.dot(a, b, precision=lax.Precision.HIGHEST, preferred_element_type=jnp.float32)


def partner(me, step):
    step = lax.rem(step * 37, 64)
    y = lax.rem(me // 16 + step // 16, 4)
    x = lax.rem(lax.rem(me // 4, 4) + lax.rem(step // 4, 4), 4)
    return y * 16 + x * 4 + jnp.bitwise_xor(lax.rem(me, 4), lax.rem(step, 4))


def remote(source, target, send, recv, device):
    pltpu.make_async_remote_copy(
        src_ref=source, dst_ref=target, send_sem=send, recv_sem=recv, device_id=device, device_id_type=MESH
    ).start()


def wait_bytes(part, sem):
    pltpu.make_async_copy(part, part, sem).wait()


def kernel(
    tables_hbm, occupations_ref, psi_hbm, rest_hbm, ionic_hbm, acc, potential_ref,
    tables, high_ref, low_ref, psi, pen, res, back, rest, ionic, part, relay, shares, density, spectrum, lines_in, lines_out, spectrum_back,
    load_sem, small_sem, fwd_send, fwd_recv, bwd_send, bwd_recv, small_send, small_recv,
):
    band, me = lax.axis_index("band"), lax.axis_index("slab")
    points = psi.shape[-1]
    barrier = pltpu.get_barrier_semaphore()

    @pl.loop(1, 64)
    def _(step):
        pl.semaphore_signal(barrier, inc=1, device_id=(band, partner(me, step)), device_id_type=MESH)

    for step in range(1, 4):
        pl.semaphore_signal(barrier, inc=1, device_id=(lax.rem(band + step, 4), me), device_id_type=MESH)

    basis_ref, basis_t_ref = tables.at[0], tables.at[1]
    def load(c):
        for group in range(4):
            o = group * 4 + c
            pltpu.make_async_copy(psi_hbm.at[:, o], psi.at[:, o], load_sem.at[c]).start()

    for c in range(CHUNKS):
        load(c)
    load_rest = pltpu.make_async_copy(rest_hbm, rest, small_sem.at[0])
    load_rest.start()
    load_tables = pltpu.make_async_copy(tables_hbm, tables, small_sem.at[2])
    load_tables.start()
    load_ionic = pltpu.make_async_copy(ionic_hbm, ionic, small_sem.at[1])
    load_ionic.start()
    wait_bytes(pen.at[0], load_sem.at[0])
    pl.semaphore_wait(barrier, 66)

    def field_part(ref, owner, c):
        rows = pl.ds(pl.multiple_of(owner // 4 * 8, 8), 8)
        return ref.at[:, lax.rem(owner, 4) * 4 + c, :, rows, :]

    def forward(c):
        @pl.loop(1, 64)
        def _(step):
            other = partner(me, step)
            remote(field_part(psi, other, c), pen.at[c, :, me], fwd_send.at[c], fwd_recv.at[c], (band, other))

        pltpu.make_async_copy(field_part(psi, me, c), pen.at[c, :, me], fwd_recv.at[c]).start()

    def backward(c):
        @pl.loop(1, 64)
        def _(step):
            other = partner(me, step)
            remote(res.at[c, :, other], field_part(back, me, c), bwd_send.at[c], bwd_recv.at[c], (band, other))

        pltpu.make_async_copy(res.at[c, :, me], field_part(back, me, c), bwd_recv.at[c]).start()

    def lines(c):
        wait_bytes(pen.at[c], fwd_recv.at[c])
        source, target = pen.reshape(CHUNKS, 2, 8 * points, points), res.reshape(CHUNKS, 2, 8 * points, points)
        for row in range(8):
            rows = pl.ds(row, points, stride=8)
            values = jnp.concatenate([source[c, 0, rows, :], source[c, 1, rows, :]], 1)
            values = left(high_ref[...], low_ref[...], values)
            target[c, 0, rows, :] = values[:, :points]
            target[c, 1, rows, :] = values[:, points:]

    def planes(c):
        @pl.loop(0, 8)
        def _(i):
            o, x = i // 2 * 4 + c, lax.rem(i, 2)
            real, imag = psi[0, o, x], psi[1, o, x]
            along_y = left(high_ref[...], low_ref[...], jnp.concatenate([real, imag], 1))
            along_z = right(jnp.concatenate([real, imag], 0), high_ref[...], low_ref[...])
            acc[0, o, x] = along_y[:, :points] + along_z[:points]
            acc[1, o, x] = along_y[:, points:] + along_z[points:]

    def finish(c):
        wait_bytes(pen.at[c], bwd_recv.at[c])

        @pl.loop(0, 8)
        def _(i):
            o, x = i // 2 * 4 + c, lax.rem(i, 2)
            potential = potential_ref[x]
            real = acc[0, o, x] + back[0, o, x] + potential * psi[0, o, x]
            imag = acc[1, o, x] + back[1, o, x] + potential * psi[1, o, x]
            acc[0, o, x] = time_step * imag
            acc[1, o, x] = -time_step * real

    after, before, across = lax.rem(band + 1, 4), lax.rem(band + 3, 4), lax.rem(band + 2, 4)

    def rows_of(owner, start, size):
        return pl.ds(pl.multiple_of(owner * 32 + start, 16), size)

    def rows_in(ref, owner, start, size):
        return ref.at[:, rows_of(owner, start, size), :]

    def density_share():
        @pl.loop(0, 8)
        def _(i):
            x, rows = i // 4, pl.ds(pl.multiple_of(lax.rem(i, 4) * 32, 32), 32)
            total = jnp.zeros((32, points), jnp.float32)
            for o in range(16):
                real, imag = psi[0, o, x, rows, :], psi[1, o, x, rows, :]
                total = total + occupations_ref[o] * (real * real + imag * imag)
            part[x, rows, :] = total

        remote(rows_in(part, across, 0, 16), relay.at[0], small_send.at[0], small_recv.at[0], (after, me))
        remote(rows_in(part, across, 16, 16), relay.at[1], small_send.at[0], small_recv.at[0], (before, me))

    def density_relay():
        wait_bytes(relay, small_recv.at[0])
        first, second = rows_of(after, 0, 16), rows_of(before, 16, 16)
        part[:, first, :] = part[:, first, :] + relay[0]
        part[:, second, :] = part[:, second, :] + relay[1]
        remote(rows_in(part, after, 0, 32), shares.at[0], small_send.at[1], small_recv.at[1], (after, me))
        remote(rows_in(part, before, 0, 32), shares.at[1], small_send.at[1], small_recv.at[1], (before, me))

    def density_sum():
        wait_bytes(shares, small_recv.at[1])
        load_rest.wait()
        rows = rows_of(band, 0, 32)
        density[:, rows, :] = rest[:, rows, :] + (part[:, rows, :] + shares[0] + shares[1])
        own = rows_in(density, band, 0, 32)
        remote(own, own, small_send.at[2], small_recv.at[2], (after, me))
        remote(own, own, small_send.at[2], small_recv.at[2], (before, me))

    def density_spread():
        wait_bytes(shares, small_recv.at[2])
        first, second = rows_in(density, before, 0, 16), rows_in(density, after, 16, 16)
        remote(first, first, small_send.at[3], small_recv.at[3], (after, me))
        remote(second, second, small_send.at[3], small_recv.at[3], (before, me))

    def owner_of(block):
        return block * 4 + lax.rem(block, 4)

    block = me // 4
    owns = owner_of(block) == me

    def block_of(ref, i):
        return ref.at[:, pl.ds(pl.multiple_of(i * 8, 8), 8), :]

    def spectrum_send():
        wait_bytes(relay, small_recv.at[3])
        half = exact(density[...].reshape(2 * points, points), basis_t_ref[...])
        both = exact(basis_ref[...], jnp.concatenate([half[:points], half[points:]], 1))
        spectrum[0] = both[:, :points]
        spectrum[1] = both[:, points:]

        @pl.loop(0, 16)
        def _(i):
            i = lax.rem(i + block, 16)
            owner = owner_of(i)

            @pl.when(owner != me)
            def _():
                remote(block_of(spectrum, i), lines_in.at[me], small_send.at[4], small_recv.at[4], (band, owner))

            @pl.when(owner == me)
            def _():
                pltpu.make_async_copy(block_of(spectrum, i), lines_in.at[me], small_recv.at[4]).start()

    def hartree_lines():
        @pl.when(owns)
        def _():
            wait_bytes(lines_in, small_recv.at[4])
            source, target = lines_in.reshape(8 * points, points), lines_out.reshape(8 * points, points)

            def folded(i):
                return jnp.minimum(i, points - i)

            kx = folded(lax.broadcasted_iota(jnp.int32, (points, points), 0))
            kz = folded(lax.broadcasted_iota(jnp.int32, (points, points), 1))
            unit = 4.0 * math.pi * (points * grid_spacing / (2.0 * math.pi)) ** 2

            def green(row):
                ky = folded(block * 8 + row)
                square = kx * kx + kz * kz + ky * ky
                return jnp.where(square > 0, unit / jnp.maximum(square, 1).astype(jnp.float32), 0.0)

            for row in range(0, 8, 2):
                first, second = pl.ds(row, points, stride=8), pl.ds(row + 1, points, stride=8)
                values = exact(basis_ref[...], jnp.concatenate([source[first, :], source[second, :]], 1))
                values = values * jnp.concatenate([green(row), green(row + 1)], 1)
                values = exact(basis_t_ref[...], values)
                target[first, :] = values[:, :points]
                target[second, :] = values[:, points:]

            @pl.loop(1, 64)
            def _(step):
                other = partner(me, step)
                remote(lines_out.at[other], block_of(spectrum_back, block), small_send.at[5], small_recv.at[5], (band, other))

            pltpu.make_async_copy(lines_out.at[me], block_of(spectrum_back, block), small_recv.at[5]).start()

    def potential_sum():
        wait_bytes(spectrum_back, small_recv.at[5])
        half = exact(spectrum_back[...].reshape(2 * points, points), basis_ref[...])
        both = exact(basis_t_ref[...], jnp.concatenate([half[:points], half[points:]], 1))
        load_ionic.wait()
        for x in range(2):
            here = density[x]
            root = jnp.exp(jnp.log(here) * (1.0 / 3.0))
            root = root - (root * root * root - here) / (3.0 * root * root)
            potential_ref[x] = ionic[x] + both[:, x * points : (x + 1) * points] - exchange_factor * root

    forward(0)
    for c in range(1, CHUNKS):
        wait_bytes(pen.at[0], load_sem.at[c])
    load_tables.wait()
    high_ref[...], low_ref[...] = split(tables[2])
    density_share()
    forward(1)
    planes(0)
    density_relay()
    forward(2)
    planes(1)
    density_sum()
    forward(3)
    planes(2)
    density_spread()
    lines(0)
    backward(0)
    planes(3)
    spectrum_send()
    lines(1)
    backward(1)
    hartree_lines()
    lines(2)
    backward(2)
    lines(3)
    backward(3)
    potential_sum()
    finish(0)
    finish(1)
    finish(2)
    finish(3)
    for c in range(CHUNKS):
        wait_bytes(pen.at[c, :, pl.ds(0, 63)], fwd_send.at[c])
        wait_bytes(pen.at[c, :, pl.ds(0, 63)], bwd_send.at[c])
    wait_bytes(relay, small_send.at[0])
    wait_bytes(shares, small_send.at[1])
    wait_bytes(shares, small_send.at[2])
    wait_bytes(relay, small_send.at[3])

    @pl.when(owns)
    def _():
        wait_bytes(lines_in.at[pl.ds(0, 15)], small_send.at[4])
        wait_bytes(lines_in.at[pl.ds(0, 63)], small_send.at[5])

    @pl.when(jnp.logical_not(owns))
    def _():
        wait_bytes(lines_in.at[pl.ds(0, 16)], small_send.at[4])


def pass_on(applied, potential, out_hbm, potential_out_hbm, sems):
    copies = [
        pltpu.make_async_copy(applied.at[p, pl.ds(o, 4)], out_hbm.at[p, pl.ds(o, 4)], sems.at[p * 4 + o // 4])
        for p in range(2)
        for o in range(0, 16, 4)
    ]
    copies.append(pltpu.make_async_copy(potential, potential_out_hbm, sems.at[8]))
    for copy in copies:
        copy.start()
    for copy in copies:
        copy.wait()


def local(orbitals, occupations, rest_density, ionic_potential):
    points = orbitals.shape[3]
    basis = real_basis(points)
    tables = np.stack([basis, basis.T, kinetic_matrix(points)])
    slab_shape = rest_density.shape
    field, slab = pltpu.VMEM(orbitals.shape, jnp.float32), pltpu.VMEM(slab_shape, jnp.float32)
    pencil = pltpu.VMEM((CHUNKS, 2, 64, 2, 8, points), jnp.float32)
    lines = pltpu.VMEM((64, 2, 8, points), jnp.float32)
    dma = pltpu.SemaphoreType.DMA
    in_vmem, anywhere = pl.BlockSpec(memory_space=pltpu.VMEM), pl.BlockSpec(memory_space=pl.ANY)
    applied, potential = pl.pallas_call(
        kernel,
        out_shape=(
            pltpu.VMEM(orbitals.shape, jnp.float32),
            pltpu.VMEM(slab_shape, jnp.float32),
        ),
        in_specs=[anywhere, pl.BlockSpec(memory_space=pltpu.SMEM), anywhere, anywhere, anywhere],
        out_specs=(in_vmem, in_vmem),
        scratch_shapes=[
            pltpu.VMEM(tables.shape, jnp.float32),
            pltpu.VMEM((points, points), jnp.bfloat16), pltpu.VMEM((points, points), jnp.bfloat16), field, pencil, pencil, field, slab, slab, slab,
            pltpu.VMEM((2, 2, 16, points), jnp.float32), pltpu.VMEM((2, 2, 32, points), jnp.float32), slab, slab, lines, lines, slab,
            dma((CHUNKS,)), dma((3,)), dma((CHUNKS,)), dma((CHUNKS,)), dma((CHUNKS,)), dma((CHUNKS,)), dma((6,)), dma((6,)),
        ],
        compiler_params=pltpu.CompilerParams(collective_id=0, has_side_effects=True, vmem_limit_bytes=58 * 2**20),
        cost_estimate=pl.CostEstimate(flops=10**10, bytes_accessed=2**25, transcendentals=0),
    )(
        jnp.asarray(tables, jnp.float32), occupations, orbitals, rest_density, ionic_potential,
    )
    return pl.pallas_call(
        pass_on,
        out_shape=(
            jax.ShapeDtypeStruct(orbitals.shape, jnp.float32),
            jax.ShapeDtypeStruct(slab_shape, jnp.float32),
        ),
        in_specs=[anywhere] * 2,
        out_specs=(anywhere, anywhere),
        scratch_shapes=[dma((9,))],
        compiler_params=pltpu.CompilerParams(vmem_limit_bytes=2**20),
    )(applied, potential)


def solution(mesh):
    return jax.shard_map(
        local,
        mesh=mesh,
        in_specs=(
            P(None, "band", "slab", None, None),
            P("band"),
            P("slab", None, None),
            P("slab", None, None),
        ),
        out_specs=(P(None, "band", "slab", None, None), P("slab", None, None)),
        check_vma=False,
    )
```

profile of v0, /device:TPU:1, one launch (start us, length us, event | category | flops | bytes accessed | tf_op | source)
XLA Modules:
  0.0 119.3 jit_solution(4991977995524015745)
XLA Ops:
  0.6 116.5 %shard_map.68 = (f32[2,16,2,128,128]{4,3,2,1,0:T(8,128)S(1)}, f32[2,128,128]{2,1,0:T(8,128)S(1)}) custom-call(f32[3,128,128]{2,1,0:T(8,128)} %constant.2.clone.tables_hbm, f32[16]{0:T(128)} %occupations_ref.1, f32[2,16,2,128,128]{4,3,2,1,0:T(8,128)} %psi_hbm.1, f32[2,128,128]{2,1,0:T(8,128)} %rest_hbm.1, f32[2,128,128]{2,1,0:T(8,128)} %ionic_hbm.1), custom_call_target="tpu_custom_call" | custom-call | flops 10000000000 | bytes 33554432 | tf_op jit(solution)/shard_map/pallas_call | solution.py:353
  117.2 2.1 %shard_map.69 = (f32[2,16,2,128,128]{4,3,2,1,0:T(8,128)}, f32[2,128,128]{2,1,0:T(8,128)}) custom-call(f32[2,16,2,128,128]{4,3,2,1,0:T(8,128)S(1)} %get-tuple-element.4.applied, f32[2,128,128]{2,1,0:T(8,128)S(1)} %get-tuple-element.5.potential), custom_call_target="tpu_custom_call" | custom-call | tf_op jit(solution)/shard_map/pallas_call | solution.py:372
where the time goes:
time: 119 us
  Pallas kernels  119 us (100%)
    pallas_call x1, Pallas kernels, local(): pl.pallas_call(kernel, out_shape=(pltpu.VMEM(orbitals.shape, jnp.float32)...  117 us

commit v1 on v0

--- a/solution.py
+++ b/solution.py
@@ -60,10 +60,10 @@
 
 
 def partner(me, step):
-    step = lax.rem(step * 37, 64)
-    y = lax.rem(me // 16 + step // 16, 4)
-    x = lax.rem(lax.rem(me // 4, 4) + lax.rem(step // 4, 4), 4)
-    return y * 16 + x * 4 + jnp.bitwise_xor(lax.rem(me, 4), lax.rem(step, 4))
+    step = (step * 37) & 63
+    y = (me + (step & 48)) & 48
+    x = (me + (step & 12)) & 12
+    return y | x | ((me ^ step) & 3)
 
 
 def remote(source, target, send, recv, device):
@@ -85,7 +85,7 @@
     points = psi.shape[-1]
     barrier = pltpu.get_barrier_semaphore()
 
-    @pl.loop(1, 64)
+    @pl.loop(1, 64, unroll=7)
     def _(step):
         pl.semaphore_signal(barrier, inc=1, device_id=(band, partner(me, step)), device_id_type=MESH)
 
@@ -110,11 +110,11 @@
     pl.semaphore_wait(barrier, 66)
 
     def field_part(ref, owner, c):
-        rows = pl.ds(pl.multiple_of(owner // 4 * 8, 8), 8)
-        return ref.at[:, lax.rem(owner, 4) * 4 + c, :, rows, :]
+        rows = pl.ds(pl.multiple_of((owner >> 2) * 8, 8), 8)
+        return ref.at[:, (owner & 3) * 4 + c, :, rows, :]
 
     def forward(c):
-        @pl.loop(1, 64)
+        @pl.loop(1, 64, unroll=7)
         def _(step):
             other = partner(me, step)
             remote(field_part(psi, other, c), pen.at[c, :, me], fwd_send.at[c], fwd_recv.at[c], (band, other))
@@ -122,7 +122,7 @@
         pltpu.make_async_copy(field_part(psi, me, c), pen.at[c, :, me], fwd_recv.at[c]).start()
 
     def backward(c):
-        @pl.loop(1, 64)
+        @pl.loop(1, 64, unroll=7)
         def _(step):
             other = partner(me, step)
             remote(res.at[c, :, other], field_part(back, me, c), bwd_send.at[c], bwd_recv.at[c], (band, other))
@@ -260,7 +260,7 @@
                 target[first, :] = values[:, :points]
                 target[second, :] = values[:, points:]
 
-            @pl.loop(1, 64)
+            @pl.loop(1, 64, unroll=7)
             def _(step):
                 other = partner(me, step)
                 remote(lines_out.at[other], block_of(spectrum_back, block), small_send.at[5], small_recv.at[5], (band, other))
@@ -285,21 +285,21 @@
     high_ref[...], low_ref[...] = split(tables[2])
     density_share()
     forward(1)
+    density_relay()
     planes(0)
-    density_relay()
     forward(2)
+    density_sum()
     planes(1)
-    density_sum()
     forward(3)
+    density_spread()
     planes(2)
-    density_spread()
     lines(0)
     backward(0)
-    planes(3)
     spectrum_send()
     lines(1)
     backward(1)
     hartree_lines()
+    planes(3)
     lines(2)
     backward(2)
     lines(3)

time: 119 us -> 118 us (level)
  Pallas kernels: 119 us -> 117 us
    pallas_call x1, Pallas kernels: 117 us -> 115 us  [local(): pl.pallas_call(kernel, out_shape=(pltpu.VMEM(orbitals.shape, jnp.float32)...]
where the time goes in v1:
time: 118 us
  Pallas kernels  117 us (99%)
    pallas_call x1, Pallas kernels, local(): pl.pallas_call(kernel, out_shape=(pltpu.VMEM(orbitals.shape, jnp.float32)...  115 us

profile of v1, /device:TPU:1, one launch (start us, length us, event | category | flops | bytes accessed | tf_op | source)
XLA Modules:
  0.0 117.6 jit_solution(10975023687171392859)
XLA Ops:
  0.6 114.9 %shard_map.68 = (f32[2,16,2,128,128]{4,3,2,1,0:T(8,128)S(1)}, f32[2,128,128]{2,1,0:T(8,128)S(1)}) custom-call(f32[3,128,128]{2,1,0:T(8,128)} %constant.2.clone.tables_hbm, f32[16]{0:T(128)} %occupations_ref.1, f32[2,16,2,128,128]{4,3,2,1,0:T(8,128)} %psi_hbm.1, f32[2,128,128]{2,1,0:T(8,128)} %rest_hbm.1, f32[2,128,128]{2,1,0:T(8,128)} %ionic_hbm.1), custom_call_target="tpu_custom_call" | custom-call | flops 10000000000 | bytes 33554432 | tf_op jit(solution)/shard_map/pallas_call | solution.py:353
  115.5 2.1 %shard_map.69 = (f32[2,16,2,128,128]{4,3,2,1,0:T(8,128)}, f32[2,128,128]{2,1,0:T(8,128)}) custom-call(f32[2,16,2,128,128]{4,3,2,1,0:T(8,128)S(1)} %get-tuple-element.4.applied, f32[2,128,128]{2,1,0:T(8,128)S(1)} %get-tuple-element.5.potential), custom_call_target="tpu_custom_call" | custom-call | tf_op jit(solution)/shard_map/pallas_call | solution.py:372

commit v2 on v1

--- a/solution.py
+++ b/solution.py
@@ -45,13 +45,15 @@
     return jnp.dot(a, b, preferred_element_type=jnp.float32)
 
 
+def left_split(matrix_high, matrix_low, high, low):
+    return dot(jnp.concatenate([matrix_high, matrix_high], 1), jnp.concatenate([high, low], 0)) + dot(matrix_low, high)
+
+
 def left(matrix_high, matrix_low, values):
-    high, low = split(values)
-    return dot(jnp.concatenate([matrix_high, matrix_high], 1), jnp.concatenate([high, low], 0)) + dot(matrix_low, high)
-
-
-def right(values, matrix_high, matrix_low):
-    high, low = split(values)
+    return left_split(matrix_high, matrix_low, *split(values))
+
+
+def right_split(high, low, matrix_high, matrix_low):
     return dot(jnp.concatenate([high, low], 1), jnp.concatenate([matrix_high, matrix_high], 0)) + dot(high, matrix_low)
 
 
@@ -144,8 +146,10 @@
         def _(i):
             o, x = i // 2 * 4 + c, lax.rem(i, 2)
             real, imag = psi[0, o, x], psi[1, o, x]
-            along_y = left(high_ref[...], low_ref[...], jnp.concatenate([real, imag], 1))
-            along_z = right(jnp.concatenate([real, imag], 0), high_ref[...], low_ref[...])
+            real_high, real_low = split(real)
+            imag_high, imag_low = split(imag)
+            along_y = left_split(high_ref[...], low_ref[...], jnp.concatenate([real_high, imag_high], 1), jnp.concatenate([real_low, imag_low], 1))
+            along_z = right_split(jnp.concatenate([real_high, imag_high], 0), jnp.concatenate([real_low, imag_low], 0), high_ref[...], low_ref[...])
             acc[0, o, x] = along_y[:, :points] + along_z[:points]
             acc[1, o, x] = along_y[:, points:] + along_z[points:]
 

time: 118 us -> 118 us (level)
  no operation moved by 1% of the time
where the time goes in v2:
time: 118 us
  Pallas kernels  117 us (99%)
    pallas_call x1, Pallas kernels, local(): pl.pallas_call(kernel, out_shape=(pltpu.VMEM(orbitals.shape, jnp.float32)...  115 us

profile of v2, /device:TPU:1, one launch (start us, length us, event | category | flops | bytes accessed | tf_op | source)
XLA Modules:
  0.0 117.6 jit_solution(10975023687171392859)
XLA Ops:
  0.6 114.9 %shard_map.68 = (f32[2,16,2,128,128]{4,3,2,1,0:T(8,128)S(1)}, f32[2,128,128]{2,1,0:T(8,128)S(1)}) custom-call(f32[3,128,128]{2,1,0:T(8,128)} %constant.2.clone.tables_hbm, f32[16]{0:T(128)} %occupations_ref.1, f32[2,16,2,128,128]{4,3,2,1,0:T(8,128)} %psi_hbm.1, f32[2,128,128]{2,1,0:T(8,128)} %rest_hbm.1, f32[2,128,128]{2,1,0:T(8,128)} %ionic_hbm.1), custom_call_target="tpu_custom_call" | custom-call | flops 10000000000 | bytes 33554432 | tf_op jit(solution)/shard_map/pallas_call | solution.py:357
  115.5 2.1 %shard_map.69 = (f32[2,16,2,128,128]{4,3,2,1,0:T(8,128)}, f32[2,128,128]{2,1,0:T(8,128)}) custom-call(f32[2,16,2,128,128]{4,3,2,1,0:T(8,128)S(1)} %get-tuple-element.4.applied, f32[2,128,128]{2,1,0:T(8,128)S(1)} %get-tuple-element.5.potential), custom_call_target="tpu_custom_call" | custom-call | tf_op jit(solution)/shard_map/pallas_call | solution.py:376
